TPU v7x, 32 devices: a whole 2x2x4 slice. The times are simulated.
32 devices in a mesh: axial: 8 (over y, x, core), trans: 4 (over z).
Axes of the slice: x: 2, y: 2, z: 4, core: 2. Of those that a mesh axis runs over, the one named last changes fastest.
Arguments:
- concentration: float32 [128, 32, 256], P('axial', 'trans'), may hold values from -4 to 4
- pore_mask: int32 [128, 32, 256], P('axial', 'trans'), may hold values 0 or 1
- velocity: float32 [128, 32, 256], P('axial', 'trans'), may hold values from 20 to 80
Outputs:
- new_concentration: float32 [128, 32, 256], P('axial', 'trans')
All inputs are finite; a program needn't handle non-finite values. No bound on the sum of `pore_mask` on one device may be relied on, other than what follows from the above.
Results may differ from a plain program's by a relative error of at most 0.00028.
Values sent between devices are 32-bit elements; how exact they have to be, the bound alone decides.
A program may use at most 64 MiB of HBM per device.

v0:
```python
import jax
import jax.numpy as jnp
from jax import lax
from jax.sharding import PartitionSpec as P

axial_number = 800.0
trans_number = 0.5


def padded(cells, sides, width):
    for axis, dim in sides:
        count = lax.axis_size(axis)
        ends = count - 1
        head = lax.slice_in_dim(cells, 0, width, axis=dim)
        tail = lax.slice_in_dim(cells, cells.shape[dim] - width, cells.shape[dim], axis=dim)
        cells = jnp.concatenate(
            [
                lax.ppermute(tail, axis, [(i, (i + 1) % count) for i in range(ends)]),
                cells,
                lax.ppermute(head, axis, [((i + 1) % count, i) for i in range(ends)]),
            ],
            axis=dim,
        )
    return cells


def plane_term(field_pad, phi_pad, field_data, axis_dim):
    cells = field_data.shape[axis_dim]
    face_share = 0.5 * (
        lax.slice_in_dim(phi_pad, 0, cells + 1, axis=axis_dim)
        + lax.slice_in_dim(phi_pad, 1, cells + 2, axis=axis_dim)
    )
    upper_part = lax.slice_in_dim(face_share, 1, cells + 1, axis=axis_dim) * (
        lax.slice_in_dim(field_pad, 2, cells + 2, axis=axis_dim) - field_data
    )
    lower_part = lax.slice_in_dim(face_share, 0, cells, axis=axis_dim) * (
        lax.slice_in_dim(field_pad, 0, cells, axis=axis_dim) - field_data
    )
    return upper_part + lower_part


def eliminate(below_coef, main_coef, above_coef, rhs):
    cell_count = main_coef.shape[0]
    first_src = jnp.concatenate([-below_coef[1:2], jnp.zeros_like(main_coef[2 : cell_count - 1])])
    last_src = jnp.concatenate(
        [
            jnp.zeros_like(main_coef[1 : cell_count - 2]),
            -above_coef[cell_count - 2 : cell_count - 1],
        ]
    )
    sources = jnp.stack([first_src, last_src, rhs[1 : cell_count - 1]], axis=1)

    def forward(running, row_data):
        ratios, partials = running
        below_row, main_row, above_row, source_row = row_data
        pivot_value = main_row - below_row * ratios
        new_ratios = above_row / pivot_value
        new_partials = (source_row - below_row[None] * partials) / pivot_value[None]
        return ((new_ratios, new_partials), (new_ratios, new_partials))

    start_state = (jnp.zeros_like(main_coef[0]), jnp.zeros_like(sources[0]))
    inputs_inner = (
        below_coef[1 : cell_count - 1],
        main_coef[1 : cell_count - 1],
        above_coef[1 : cell_count - 1],
        sources,
    )
    _, (ratio_rows, partial_rows) = lax.scan(forward, start_state, inputs_inner)

    def backward(next_value, row_data):
        ratios, partials = row_data
        now_value = partials - ratios[None] * next_value
        return (now_value, now_value)

    _, interior = lax.scan(
        backward, jnp.zeros_like(partial_rows[0]), (ratio_rows, partial_rows), reverse=True
    )
    last_cell = cell_count - 1
    first_lower = below_coef[0]
    first_main = main_coef[0] + above_coef[0] * interior[0, 0]
    first_upper = above_coef[0] * interior[0, 1]
    first_rhs = rhs[0] - above_coef[0] * interior[0, 2]
    last_lower = below_coef[last_cell] * interior[-1, 0]
    last_main = main_coef[last_cell] + below_coef[last_cell] * interior[-1, 1]
    last_upper = above_coef[last_cell]
    last_rhs = rhs[last_cell] - below_coef[last_cell] * interior[-1, 2]
    reduced = jnp.stack(
        [
            jnp.stack([first_lower, last_lower]),
            jnp.stack([first_main, last_main]),
            jnp.stack([first_upper, last_upper]),
            jnp.stack([first_rhs, last_rhs]),
        ]
    )
    return (reduced, interior)


def assemble(first_cell, last_cell, interior):
    inner_cells = (
        interior[:, 0] * first_cell[None] + interior[:, 1] * last_cell[None] + interior[:, 2]
    )
    return jnp.concatenate([first_cell[None], inner_cells, last_cell[None]])


def reduce_cyclic(lower_part, main_part, upper_part, right_part):
    row_count = lower_part.shape[0]
    for stride_level in range(row_count.bit_length() - 1):
        stride = 2**stride_level

        def from_lower(values, fill_value):
            return jnp.concatenate(
                [jnp.full_like(values[:stride], fill_value), values[: row_count - stride]]
            )

        def from_upper(values, fill_value):
            return jnp.concatenate([values[stride:], jnp.full_like(values[:stride], fill_value)])

        factor_low = lower_part / from_lower(main_part, 1.0)
        factor_high = upper_part / from_upper(main_part, 1.0)
        new_lower = -factor_low * from_lower(lower_part, 0.0)
        new_main = (
            main_part
            - factor_low * from_lower(upper_part, 0.0)
            - factor_high * from_upper(lower_part, 0.0)
        )
        new_upper = -factor_high * from_upper(upper_part, 0.0)
        new_right = (
            right_part
            - factor_low * from_lower(right_part, 0.0)
            - factor_high * from_upper(right_part, 0.0)
        )
        lower_part, main_part, upper_part, right_part = (new_lower, new_main, new_upper, new_right)
    return right_part / main_part


def body(concentration, pore_mask, velocity):
    porosity = 0.1 + 0.9 * pore_mask.astype(jnp.float32)
    axial_ext = padded(jnp.stack([concentration, porosity, velocity]), (("axial", 1),), 1)
    conc_ext = axial_ext[0]
    phi_ext = axial_ext[1]
    vel_ext = axial_ext[2]
    face_share = 0.5 * (phi_ext[:-1] + phi_ext[1:])
    advect = 0.5 * (vel_ext[:-1] + vel_ext[1:]) * face_share
    spread = axial_number * face_share
    lower_coef = advect[:-1] + spread[:-1]
    upper_coef = spread[1:]
    center = spread[:-1] + spread[1:] + advect[1:]
    axial_term = lower_coef * conc_ext[:-2] - center * concentration + upper_coef * conc_ext[2:]
    plane_ext = padded(jnp.stack([concentration, porosity]), (("trans", 2),), 1)
    transverse = plane_term(plane_ext[0], plane_ext[1], concentration, 1)
    z_widths = ((0, 0), (0, 0), (1, 1))
    transverse = transverse + plane_term(
        jnp.pad(concentration, z_widths), jnp.pad(porosity, z_widths), concentration, 2
    )
    rhs = concentration + axial_term + trans_number * transverse
    below_coef = -lower_coef
    main_coef = 1.0 + center
    above_coef = -upper_coef
    device_index = lax.axis_index("axial")
    reduced, interior = eliminate(below_coef, main_coef, above_coef, rhs)
    gathered = lax.all_gather(reduced, "axial", axis=1, tiled=True)
    all_ends = reduce_cyclic(gathered[0], gathered[1], gathered[2], gathered[3])
    end_values = lax.dynamic_slice_in_dim(all_ends, 2 * device_index, 2, 0)
    return assemble(end_values[0], end_values[1], interior)


def solution(mesh):
    in_specs = (P("axial", "trans", None), P("axial", "trans", None), P("axial", "trans", None))
    out_specs = P("axial", "trans", None)
    return jax.shard_map(body, mesh=mesh, in_specs=in_specs, out_specs=out_specs, check_vma=False)
```

profile of v0, /device:TPU:0, one launch (start us, length us, event | category | flops | bytes accessed | tf_op | source)
XLA Modules:
  0.0 33.0 jit_solution(11848905922522627214)
XLA Ops:
  0.0 1.0 %fusion.47 = (f32[1,16,8,256]{3,2,1,0:T(8,128)S(1)}, f32[16,8,256]{2,1,0:T(8,128)S(1)}) fusion(s32[16,8,256]{2,1,0:T(8,128)} %param.8), kind=kLoop, calls=%fused_computation.145 | loop fusion | flops 98304 | bytes 393216 | tf_op jit(solution)/shard_map/stack | solution.py:138
  1.0 0.0 copy-done.1
  1.0 2.3 %collective-permute-start = (f32[3,1,8,256]{3,2,1,0:T(8,128)S(1)}, f32[3,1,8,256]{3,2,1,0:T(8,128)S(1)}, u32[]{:S(2)}, u32[]{:S(2)}) collective-permute-start(f32[3,1,8,256]{3,2,1,0:T(8,128)S(1)} %get-tuple-element.278), channel_id=1, source_target_pairs={{0,4},{4,8},{8,12},{12,16},{16,20},{20,24},{24,28},{1,5},{5,9},{9,... | collective-permute-start | bytes 73736 | tf_op jit(solution)/shard_map/ppermute | solution.py:18
  3.4 1.3 %collective-permute-start.1 = (f32[3,1,8,256]{3,2,1,0:T(8,128)S(1)}, f32[3,1,8,256]{3,2,1,0:T(8,128)S(1)}, u32[]{:S(2)}, u32[]{:S(2)}) collective-permute-start(f32[3,1,8,256]{3,2,1,0:T(8,128)S(1)} %get-tuple-element.279), channel_id=1, source_target_pairs={{4,0},{8,4},{12,8},{16,12},{20,16},{24,20},{28,24},{5,1},{9,5},{13... | collective-permute-start | bytes 73736 | tf_op jit(solution)/shard_map/ppermute | solution.py:20
  4.7 4.3 %collective-permute-start.2 = (f32[2,16,1,256]{3,2,1,0:T(1,128)S(1)}, f32[2,16,1,256]{3,2,1,0:T(1,128)S(1)}, u32[]{:S(2)}, u32[]{:S(2)}) collective-permute-start(f32[2,16,1,256]{3,2,1,0:T(1,128)S(1)} %get-tuple-element.282), channel_id=1, source_target_pairs={{0,1},{1,2},{2,3},{4,5},{5,6},{6,7},{8,9},{9,10},{10,11},{12,13},{... | collective-permute-start | bytes 98312 | tf_op jit(solution)/shard_map/ppermute | solution.py:18
  9.1 1.3 %collective-permute-start.3 = (f32[2,16,1,256]{3,2,1,0:T(1,128)S(1)}, f32[2,16,1,256]{3,2,1,0:T(1,128)S(1)}, u32[]{:S(2)}, u32[]{:S(2)}) collective-permute-start(f32[2,16,1,256]{3,2,1,0:T(1,128)S(1)} %get-tuple-element.283), channel_id=1, source_target_pairs={{1,0},{2,1},{3,2},{5,4},{6,5},{7,6},{9,8},{10,9},{11,10},{13,12},{... | collective-permute-start | bytes 98312 | tf_op jit(solution)/shard_map/ppermute | solution.py:20
  10.4 0.1 fusion.3
  10.5 0.1 maximum_maximum_fusion
  10.8 0.6 %copy-done.2 = f32[16,8,256]{2,1,0:T(8,128)} copy-done((f32[16,8,256]{2,1,0:T(8,128)}, f32[16,8,256]{2,1,0:T(8,128)S(1)}, u32[]{:S(2)}) %copy-start.2) | copy-done | bytes 131096
  11.4 3.4 %collective-permute-done.3 = f32[2,16,1,256]{3,2,1,0:T(1,128)S(1)} collective-permute-done((f32[2,16,1,256]{3,2,1,0:T(1,128)S(1)}, f32[2,16,1,256]{3,2,1,0:T(1,128)S(1)}, u32[]{:S(2)}, u32[]{:S(2)}) %collective-permute-start.3) | collective-permute-done | bytes 32800 | tf_op jit(solution)/shard_map/ppermute | solution.py:20
  14.9 0.1 pad_maximum_fusion
  15.1 0.2 fusion.11
  15.4 0.9 %slice-done = f32[14,8,256]{2,1,0:T(8,128)S(1)} async-done(((f32[16,8,256]{2,1,0:T(8,128)}), f32[14,8,256]{2,1,0:T(8,128)S(1)}, s32[]{:S(2)}) %slice-start) | async-done | bytes 114712 | tf_op jit(solution)/shard_map/slice | solution.py:64
  16.2 0.9 %while.34 = (s32[]{:T(128)}, f32[8,256]{1,0:T(8,128)S(1)}, f32[3,8,256]{2,1,0:T(8,128)S(1)}, f32[14,8,256]{2,1,0:T(8,128)S(1)}, f32[14,3,8,256]{3,2,1,0:T(8,128)...) while((s32[]{:T(128)}, f32[8,256]{1,0:T(8,128)S(1)}, ...), condition=%wide.region_1.2_spmd.clone, body=%wide.region_0.1_spmd.clone.sunk | while | flops 32771 | bytes 180352 | solution.py:68
  17.1 0.8 %while.35 = (s32[]{:T(128)}, f32[3,8,256]{2,1,0:T(8,128)S(1)}, f32[14,3,8,256]{3,2,1,0:T(8,128)S(1)}, f32[14,3,8,256]{3,2,1,0:T(8,128)S(1)}, f32[14,8,256]{2,1,0...) while((s32[]{:T(128)}, f32[3,8,256]{2,1,0:T(8,128)S(1)}, f32[14,3,8,256]{3,2,1,0:T(8,128)S(1)}, ...), condition=%wide.region_3.4_spmd.clone, body=%wide.region_2.3_spmd.clone.sunk | while | flops 18436 | bytes 122995 | solution.py:75
  18.0 0.1 copy-done.3
  18.1 13.3 %all_gather.3 = f32[4,16,8,256]{3,2,1,0:T(8,128)S(1)} all-gather(f32[4,2,8,256]{3,2,1,0:T(8,128)S(1)} %pad_maximum_fusion.4), channel_id=1, replica_groups=mesh['axial'=8,'trans'=4] {'axial'}, dimensions={1}, use_global_device_ids=true | all-gather | bytes 589824 | tf_op jit(solution)/shard_map/all_gather | solution.py:161
  31.4 0.1 slice_bitcast_fusion.9
  31.5 0.1 fusion.15
  31.6 0.1 multiply_subtract_fusion.3
  31.8 0.1 multiply_subtract_fusion.2
  31.9 0.1 multiply_subtract_fusion.1
  32.1 0.1 pad_multiply_fusion.1
  32.3 0.7 %pad_maximum_fusion.3 = f32[16,8,256]{2,1,0:T(8,128)} fusion(f32[1,8,256]{2,1,0:T(8,128)S(1)} %get-tuple-element.316, f32[14,8,256]{2,1,0:T(8,128)S(1)} %fusion.29, f32[1,8,256]{2,1,0:T(8,128)S(1)} %get-tuple-element.313), kind=kLoop, calls=%fused_computation.64 | loop fusion | flops 65536 | bytes 262144 | tf_op jit(solution)/shard_map/concatenate | solution.py:102
  (106 shorter events, 1.4 us)
Async XLA Ops:
  0.0 1.0 %copy-start = (f32[16,8,256]{2,1,0:T(8,128)S(1)}, f32[16,8,256]{2,1,0:T(8,128)}, u32[]{:S(2)}) copy-start(f32[16,8,256]{2,1,0:T(8,128)} %param.7) | copy-start | bytes 393220
  0.0 1.0 %copy-start.1 = (f32[16,8,256]{2,1,0:T(8,128)S(1)}, f32[16,8,256]{2,1,0:T(8,128)}, u32[]{:S(2)}) copy-start(f32[16,8,256]{2,1,0:T(8,128)} %param.9) | copy-start | bytes 393220
  1.0 9.5 %collective-permute-start = (f32[3,1,8,256]{3,2,1,0:T(8,128)S(1)}, f32[3,1,8,256]{3,2,1,0:T(8,128)S(1)}, u32[]{:S(2)}, u32[]{:S(2)}) collective-permute-start(f32[3,1,8,256]{3,2,1,0:T(8,128)S(1)} %get-tuple-element.278), channel_id=1, source_target_pairs={{0,4},{4,8},{8,12},{12,16},{16,20},{20,24},{24,28},{1,5},{5,9},{9,... | collective-permute-start | bytes 73736 | tf_op jit(solution)/shard_map/ppermute | solution.py:18
  3.4 7.1 %collective-permute-start.1 = (f32[3,1,8,256]{3,2,1,0:T(8,128)S(1)}, f32[3,1,8,256]{3,2,1,0:T(8,128)S(1)}, u32[]{:S(2)}, u32[]{:S(2)}) collective-permute-start(f32[3,1,8,256]{3,2,1,0:T(8,128)S(1)} %get-tuple-element.279), channel_id=1, source_target_pairs={{4,0},{8,4},{12,8},{16,12},{20,16},{24,20},{28,24},{5,1},{9,5},{13... | collective-permute-start | bytes 73736 | tf_op jit(solution)/shard_map/ppermute | solution.py:20
  4.7 6.7 %collective-permute-start.2 = (f32[2,16,1,256]{3,2,1,0:T(1,128)S(1)}, f32[2,16,1,256]{3,2,1,0:T(1,128)S(1)}, u32[]{:S(2)}, u32[]{:S(2)}) collective-permute-start(f32[2,16,1,256]{3,2,1,0:T(1,128)S(1)} %get-tuple-element.282), channel_id=1, source_target_pairs={{0,1},{1,2},{2,3},{4,5},{5,6},{6,7},{8,9},{9,10},{10,11},{12,13},{... | collective-permute-start | bytes 98312 | tf_op jit(solution)/shard_map/ppermute | solution.py:18
  9.1 5.8 %collective-permute-start.3 = (f32[2,16,1,256]{3,2,1,0:T(1,128)S(1)}, f32[2,16,1,256]{3,2,1,0:T(1,128)S(1)}, u32[]{:S(2)}, u32[]{:S(2)}) collective-permute-start(f32[2,16,1,256]{3,2,1,0:T(1,128)S(1)} %get-tuple-element.283), channel_id=1, source_target_pairs={{1,0},{2,1},{3,2},{5,4},{6,5},{7,6},{9,8},{10,9},{11,10},{13,12},{... | collective-permute-start | bytes 98312 | tf_op jit(solution)/shard_map/ppermute | solution.py:20
  10.8 0.7 %copy-start.2 = (f32[16,8,256]{2,1,0:T(8,128)}, f32[16,8,256]{2,1,0:T(8,128)S(1)}, u32[]{:S(2)}) copy-start(f32[16,8,256]{2,1,0:T(8,128)S(1)} %broadcast_add_fusion) | copy-start | bytes 393220
  15.3 0.9 %slice-start = ((f32[16,8,256]{2,1,0:T(8,128)}), f32[14,8,256]{2,1,0:T(8,128)S(1)}, s32[]{:S(2)}) async-start(f32[16,8,256]{2,1,0:T(8,128)} %copy-done.2), calls=%async_computation | async-start | bytes 229376 | tf_op jit(solution)/shard_map/slice | solution.py:64
  17.1 0.9 %copy-start.3 = (f32[16,8,256]{2,1,0:T(8,128)S(1)}, f32[16,8,256]{2,1,0:T(8,128)}, u32[]{:S(2)}) copy-start(f32[16,8,256]{2,1,0:T(8,128)} %copy-done.2) | copy-start | bytes 393220
where the time goes:
time: 33.2 us; the launch traced here: 33 us
  blocking collectives  13.3 us (40%)
  starting transfers between devices  9.24 us (28%)
  other arithmetic  3.51 us (11%)
  waiting for transfers between devices  3.45 us (10%)
  local copies, waits for them, and re-layouts  2.09 us (6%)
  loops' own time  0.93 us (3%)
  between operations  0.44 us (1%)
    all_gather x1, blocking collectives, body(): gathered = lax.all_gather(reduced, 'axial', axis=1, tiled=True)  13.3 us
    ppermute x2, starting transfers between devices, padded(): lax.ppermute(tail, axis, [(i, (i + 1) % count) for i in range(ends)])  6.66 us
    ppermute x2, waiting for transfers between devices, padded(): lax.ppermute(head, axis, [((i + 1) % count, i) for i in range(ends)])  3.45 us
    ppermute x2, starting transfers between devices, padded(): lax.ppermute(head, axis, [((i + 1) % count, i) for i in range(ends)])  2.58 us
    another operation x1, other arithmetic, body(): jnp.stack([concentration, porosity, velocity])  0.97 us
    slice x2, local copies, waits for them, and re-layouts, eliminate(): main_coef[1:cell_count - 1]  0.86 us
    unnamed x8, local copies, waits for them, and re-layouts  0.75 us
    concatenate x1, other arithmetic, assemble(): return jnp.concatenate([first_cell[None], inner_cells, last_cell[None]])  0.67 us
  transfers between devices with their start and end apart: 4, of which 1 were waited for; matrix products, arithmetic and copies ran while one was open for 1% of the time, Pallas kernels for 0%

commit v1 on v0

--- a/solution.py
+++ b/solution.py
@@ -158,7 +158,15 @@
     above_coef = -upper_coef
     device_index = lax.axis_index("axial")
     reduced, interior = eliminate(below_coef, main_coef, above_coef, rhs)
-    gathered = lax.all_gather(reduced, "axial", axis=1, tiled=True)
+    ways, here, step = (lax.axis_size("axial"), lax.axis_index("axial"), reduced.shape[1])
+    line, have = (reduced, 1)
+    while have < ways:
+        line = jnp.concatenate(
+            [line, lax.ppermute(line, "axial", [(d, (d - have) % ways) for d in range(ways)])],
+            axis=1,
+        )
+        have = 2 * have
+    gathered = jnp.roll(line, here * step, axis=1)
     all_ends = reduce_cyclic(gathered[0], gathered[1], gathered[2], gathered[3])
     end_values = lax.dynamic_slice_in_dim(all_ends, 2 * device_index, 2, 0)
     return assemble(end_values[0], end_values[1], interior)

time: 33.2 us -> 39.6 us (1.19)
  blocking collectives: 13.3 us -> 0 us
  waiting for transfers between devices: 3.45 us -> 14.7 us
  starting transfers between devices: 9.24 us -> 17.6 us
    all_gather x1 -> x0, blocking collectives: 13.3 us -> none  [body(): gathered = lax.all_gather(reduced, 'axial', axis=1, tiled=True)]
    ppermute x0 -> x3, waiting for transfers between devices: none -> 11.2 us  [body(): lax.ppermute(line, 'axial', [(d, (d - have) % ways) for d in range(ways)])]
    ppermute x0 -> x3, starting transfers between devices: none -> 8.33 us  [body(): lax.ppermute(line, 'axial', [(d, (d - have) % ways) for d in range(ways)])]
  transfers between devices with their start and end apart: 4 -> 7, of which waited for: 1 -> 4; matrix products, arithmetic and copies ran while one was open for 1% -> 1% of each run, Pallas kernels for 0% -> 0%
where the time goes in v1:
time: 39.6 us; the launch traced here: 39.4 us
  starting transfers between devices  17.6 us (44%)
  waiting for transfers between devices  14.7 us (37%)
  other arithmetic  3.59 us (9%)
  local copies, waits for them, and re-layouts  2.13 us (5%)
  loops' own time  0.89 us (2%)
  between operations  0.5 us (1%)
    ppermute x3, waiting for transfers between devices, body(): lax.ppermute(line, 'axial', [(d, (d - have) % ways) for d in range(ways)])  11.2 us
    ppermute x3, starting transfers between devices, body(): lax.ppermute(line, 'axial', [(d, (d - have) % ways) for d in range(ways)])  8.33 us
    ppermute x2, starting transfers between devices, padded(): lax.ppermute(tail, axis, [(i, (i + 1) % count) for i in range(ends)])  6.66 us
    ppermute x2, waiting for transfers between devices, padded(): lax.ppermute(head, axis, [((i + 1) % count, i) for i in range(ends)])  3.52 us
    ppermute x2, starting transfers between devices, padded(): lax.ppermute(head, axis, [((i + 1) % count, i) for i in range(ends)])  2.58 us
    another operation x1, other arithmetic, body(): jnp.stack([concentration, porosity, velocity])  0.97 us
    slice x2, local copies, waits for them, and re-layouts, eliminate(): main_coef[1:cell_count - 1]  0.86 us
  transfers between devices with their start and end apart: 7, of which 4 were waited for; matrix products, arithmetic and copies ran while one was open for 1% of the time, Pallas kernels for 0%

profile of v1, /device:TPU:0, one launch (start us, length us, event | category | flops | bytes accessed | tf_op | source)
XLA Modules:
  0.0 39.4 jit_solution(18207865672458294698)
XLA Ops:
  0.0 1.0 %fusion.47 = (f32[1,16,8,256]{3,2,1,0:T(8,128)S(1)}, f32[16,8,256]{2,1,0:T(8,128)S(1)}) fusion(s32[16,8,256]{2,1,0:T(8,128)} %param.8), kind=kLoop, calls=%fused_computation.155 | loop fusion | flops 98304 | bytes 393216 | tf_op jit(solution)/shard_map/stack | solution.py:138
  1.0 2.3 %collective-permute-start = (f32[3,1,8,256]{3,2,1,0:T(8,128)S(1)}, f32[3,1,8,256]{3,2,1,0:T(8,128)S(1)}, u32[]{:S(2)}, u32[]{:S(2)}) collective-permute-start(f32[3,1,8,256]{3,2,1,0:T(8,128)S(1)} %get-tuple-element.278), channel_id=1, source_target_pairs={{0,4},{4,8},{8,12},{12,16},{16,20},{20,24},{24,28},{1,5},{5,9},{9,... | collective-permute-start | bytes 73736 | tf_op jit(solution)/shard_map/ppermute | solution.py:18
  3.4 1.3 %collective-permute-start.1 = (f32[3,1,8,256]{3,2,1,0:T(8,128)S(1)}, f32[3,1,8,256]{3,2,1,0:T(8,128)S(1)}, u32[]{:S(2)}, u32[]{:S(2)}) collective-permute-start(f32[3,1,8,256]{3,2,1,0:T(8,128)S(1)} %get-tuple-element.279), channel_id=1, source_target_pairs={{4,0},{8,4},{12,8},{16,12},{20,16},{24,20},{28,24},{5,1},{9,5},{13... | collective-permute-start | bytes 73736 | tf_op jit(solution)/shard_map/ppermute | solution.py:20
  4.7 4.3 %collective-permute-start.2 = (f32[2,16,1,256]{3,2,1,0:T(1,128)S(1)}, f32[2,16,1,256]{3,2,1,0:T(1,128)S(1)}, u32[]{:S(2)}, u32[]{:S(2)}) collective-permute-start(f32[2,16,1,256]{3,2,1,0:T(1,128)S(1)} %get-tuple-element.282), channel_id=1, source_target_pairs={{0,1},{1,2},{2,3},{4,5},{5,6},{6,7},{8,9},{9,10},{10,11},{12,13},{... | collective-permute-start | bytes 98312 | tf_op jit(solution)/shard_map/ppermute | solution.py:18
  9.1 1.3 %collective-permute-start.3 = (f32[2,16,1,256]{3,2,1,0:T(1,128)S(1)}, f32[2,16,1,256]{3,2,1,0:T(1,128)S(1)}, u32[]{:S(2)}, u32[]{:S(2)}) collective-permute-start(f32[2,16,1,256]{3,2,1,0:T(1,128)S(1)} %get-tuple-element.283), channel_id=1, source_target_pairs={{1,0},{2,1},{3,2},{5,4},{6,5},{7,6},{9,8},{10,9},{11,10},{13,12},{... | collective-permute-start | bytes 98312 | tf_op jit(solution)/shard_map/ppermute | solution.py:20
  10.4 0.1 fusion.3
  10.8 0.5 %copy-done.2 = f32[16,8,256]{2,1,0:T(8,128)} copy-done((f32[16,8,256]{2,1,0:T(8,128)}, f32[16,8,256]{2,1,0:T(8,128)S(1)}, u32[]{:S(2)}) %copy-start.2) | copy-done | bytes 131096
  11.4 3.5 %collective-permute-done.3 = f32[2,16,1,256]{3,2,1,0:T(1,128)S(1)} collective-permute-done((f32[2,16,1,256]{3,2,1,0:T(1,128)S(1)}, f32[2,16,1,256]{3,2,1,0:T(1,128)S(1)}, u32[]{:S(2)}, u32[]{:S(2)}) %collective-permute-start.3) | collective-permute-done | bytes 32800 | tf_op jit(solution)/shard_map/ppermute | solution.py:20
  14.9 0.1 pad_maximum_fusion
  15.1 0.2 fusion.11
  15.4 0.9 %slice-done = f32[14,8,256]{2,1,0:T(8,128)S(1)} async-done(((f32[16,8,256]{2,1,0:T(8,128)}), f32[14,8,256]{2,1,0:T(8,128)S(1)}, s32[]{:S(2)}) %slice-start) | async-done | bytes 114712 | tf_op jit(solution)/shard_map/slice | solution.py:64
  16.2 0.9 %while.34 = (s32[]{:T(128)}, f32[8,256]{1,0:T(8,128)S(1)}, f32[3,8,256]{2,1,0:T(8,128)S(1)}, f32[14,8,256]{2,1,0:T(8,128)S(1)}, f32[14,3,8,256]{3,2,1,0:T(8,128)...) while((s32[]{:T(128)}, f32[8,256]{1,0:T(8,128)S(1)}, ...), condition=%wide.region_1.2_spmd.clone, body=%wide.region_0.1_spmd.clone.sunk | while | flops 32771 | bytes 180360 | solution.py:68
  17.1 0.8 %while.35 = (s32[]{:T(128)}, f32[3,8,256]{2,1,0:T(8,128)S(1)}, f32[14,3,8,256]{3,2,1,0:T(8,128)S(1)}, f32[14,3,8,256]{3,2,1,0:T(8,128)S(1)}, f32[14,8,256]{2,1,0...) while((s32[]{:T(128)}, f32[3,8,256]{2,1,0:T(8,128)S(1)}, f32[14,3,8,256]{3,2,1,0:T(8,128)S(1)}, ...), condition=%wide.region_3.4_spmd.clone, body=%wide.region_2.3_spmd.clone.sunk | while | flops 18436 | bytes 123003 | solution.py:75
  18.1 2.0 %collective-permute-start.4 = (f32[4,2,8,256]{3,2,1,0:T(8,128)S(1)}, f32[4,2,8,256]{3,2,1,0:T(8,128)S(1)}, u32[]{:S(2)}, u32[]{:S(2)}) collective-permute-start(f32[4,2,8,256]{3,2,1,0:T(8,128)S(1)} %get-tuple-element.313), channel_id=1, source_target_pairs={{0,28},{4,0},{8,4},{12,8},{16,12},{20,16},{24,20},{28,24},{1,29},{... | collective-permute-start | bytes 196616 | tf_op jit(solution)/shard_map/ppermute | solution.py:165
  20.1 1.9 %collective-permute-done.4 = f32[4,2,8,256]{3,2,1,0:T(8,128)S(1)} collective-permute-done((f32[4,2,8,256]{3,2,1,0:T(8,128)S(1)}, f32[4,2,8,256]{3,2,1,0:T(8,128)S(1)}, u32[]{:S(2)}, u32[]{:S(2)}) %collective-permute-start.4) | collective-permute-done | bytes 65568 | tf_op jit(solution)/shard_map/ppermute | solution.py:165
  22.0 3.1 %collective-permute-start.5 = (f32[4,4,8,256]{3,2,1,0:T(8,128)S(1)}, f32[4,4,8,256]{3,2,1,0:T(8,128)S(1)}, u32[]{:S(2)}, u32[]{:S(2)}) collective-permute-start(f32[4,4,8,256]{3,2,1,0:T(8,128)S(1)} %pad_maximum_fusion.4), channel_id=1, source_target_pairs={{0,24},{4,28},{8,0},{12,4},{16,8},{20,12},{24,16},{28,20},{1,25},{... | collective-permute-start | bytes 393224 | tf_op jit(solution)/shard_map/ppermute | solution.py:165
  25.1 2.9 %collective-permute-done.5 = f32[4,4,8,256]{3,2,1,0:T(8,128)S(1)} collective-permute-done((f32[4,4,8,256]{3,2,1,0:T(8,128)S(1)}, f32[4,4,8,256]{3,2,1,0:T(8,128)S(1)}, u32[]{:S(2)}, u32[]{:S(2)}) %collective-permute-start.5) | collective-permute-done | bytes 131104 | tf_op jit(solution)/shard_map/ppermute | solution.py:165
  28.1 3.2 %collective-permute-start.6 = (f32[4,8,8,256]{3,2,1,0:T(8,128)S(1)}, f32[4,8,8,256]{3,2,1,0:T(8,128)S(1)}, u32[]{:S(2)}, u32[]{:S(2)}) collective-permute-start(f32[4,8,8,256]{3,2,1,0:T(8,128)S(1)} %pad_maximum_fusion.3), channel_id=1, source_target_pairs={{0,16},{4,20},{8,24},{12,28},{16,0},{20,4},{24,8},{28,12},{1,17},{... | collective-permute-start | bytes 786440 | tf_op jit(solution)/shard_map/ppermute | solution.py:165
  31.4 6.3 %collective-permute-done.6 = f32[4,8,8,256]{3,2,1,0:T(8,128)S(1)} collective-permute-done((f32[4,8,8,256]{3,2,1,0:T(8,128)S(1)}, f32[4,8,8,256]{3,2,1,0:T(8,128)S(1)}, u32[]{:S(2)}, u32[]{:S(2)}) %collective-permute-start.6) | collective-permute-done | bytes 262176 | tf_op jit(solution)/shard_map/ppermute | solution.py:165
  37.8 0.1 dynamic-slice_bitcast_fusion.9
  37.9 0.1 fusion.15
  38.1 0.1 multiply_subtract_fusion.3
  38.4 0.1 multiply_subtract_fusion.1
  38.7 0.7 %pad_maximum_fusion.5 = f32[16,8,256]{2,1,0:T(8,128)} fusion(f32[1,8,256]{2,1,0:T(8,128)S(1)} %get-tuple-element.318, f32[14,8,256]{2,1,0:T(8,128)S(1)} %fusion.29, f32[1,8,256]{2,1,0:T(8,128)S(1)} %get-tuple-element.315), kind=kLoop, calls=%fused_computation.66 | loop fusion | flops 65536 | bytes 262144 | tf_op jit(solution)/shard_map/concatenate | solution.py:102
  (120 shorter events, 1.9 us)
Async XLA Ops:
  0.0 1.0 %copy-start = (f32[16,8,256]{2,1,0:T(8,128)S(1)}, f32[16,8,256]{2,1,0:T(8,128)}, u32[]{:S(2)}) copy-start(f32[16,8,256]{2,1,0:T(8,128)} %param.7) | copy-start | bytes 393220
  0.0 1.0 %copy-start.1 = (f32[16,8,256]{2,1,0:T(8,128)S(1)}, f32[16,8,256]{2,1,0:T(8,128)}, u32[]{:S(2)}) copy-start(f32[16,8,256]{2,1,0:T(8,128)} %param.9) | copy-start | bytes 393220
  1.0 9.5 %collective-permute-start = (f32[3,1,8,256]{3,2,1,0:T(8,128)S(1)}, f32[3,1,8,256]{3,2,1,0:T(8,128)S(1)}, u32[]{:S(2)}, u32[]{:S(2)}) collective-permute-start(f32[3,1,8,256]{3,2,1,0:T(8,128)S(1)} %get-tuple-element.278), channel_id=1, source_target_pairs={{0,4},{4,8},{8,12},{12,16},{16,20},{20,24},{24,28},{1,5},{5,9},{9,... | collective-permute-start | bytes 73736 | tf_op jit(solution)/shard_map/ppermute | solution.py:18
  3.4 7.1 %collective-permute-start.1 = (f32[3,1,8,256]{3,2,1,0:T(8,128)S(1)}, f32[3,1,8,256]{3,2,1,0:T(8,128)S(1)}, u32[]{:S(2)}, u32[]{:S(2)}) collective-permute-start(f32[3,1,8,256]{3,2,1,0:T(8,128)S(1)} %get-tuple-element.279), channel_id=1, source_target_pairs={{4,0},{8,4},{12,8},{16,12},{20,16},{24,20},{28,24},{5,1},{9,5},{13... | collective-permute-start | bytes 73736 | tf_op jit(solution)/shard_map/ppermute | solution.py:20
  4.7 6.6 %collective-permute-start.2 = (f32[2,16,1,256]{3,2,1,0:T(1,128)S(1)}, f32[2,16,1,256]{3,2,1,0:T(1,128)S(1)}, u32[]{:S(2)}, u32[]{:S(2)}) collective-permute-start(f32[2,16,1,256]{3,2,1,0:T(1,128)S(1)} %get-tuple-element.282), channel_id=1, source_target_pairs={{0,1},{1,2},{2,3},{4,5},{5,6},{6,7},{8,9},{9,10},{10,11},{12,13},{... | collective-permute-start | bytes 98312 | tf_op jit(solution)/shard_map/ppermute | solution.py:18
  9.1 5.8 %collective-permute-start.3 = (f32[2,16,1,256]{3,2,1,0:T(1,128)S(1)}, f32[2,16,1,256]{3,2,1,0:T(1,128)S(1)}, u32[]{:S(2)}, u32[]{:S(2)}) collective-permute-start(f32[2,16,1,256]{3,2,1,0:T(1,128)S(1)} %get-tuple-element.283), channel_id=1, source_target_pairs={{1,0},{2,1},{3,2},{5,4},{6,5},{7,6},{9,8},{10,9},{11,10},{13,12},{... | collective-permute-start | bytes 98312 | tf_op jit(solution)/shard_map/ppermute | solution.py:20
  10.7 0.7 %copy-start.2 = (f32[16,8,256]{2,1,0:T(8,128)}, f32[16,8,256]{2,1,0:T(8,128)S(1)}, u32[]{:S(2)}) copy-start(f32[16,8,256]{2,1,0:T(8,128)S(1)} %broadcast_add_fusion) | copy-start | bytes 393220
  15.3 0.9 %slice-start = ((f32[16,8,256]{2,1,0:T(8,128)}), f32[14,8,256]{2,1,0:T(8,128)S(1)}, s32[]{:S(2)}) async-start(f32[16,8,256]{2,1,0:T(8,128)} %copy-done.2), calls=%async_computation | async-start | bytes 229376 | tf_op jit(solution)/shard_map/slice | solution.py:64
  17.1 0.9 %copy-start.3 = (f32[16,8,256]{2,1,0:T(8,128)S(1)}, f32[16,8,256]{2,1,0:T(8,128)}, u32[]{:S(2)}) copy-start(f32[16,8,256]{2,1,0:T(8,128)} %copy-done.2) | copy-start | bytes 393220
  18.1 3.9 %collective-permute-start.4 = (f32[4,2,8,256]{3,2,1,0:T(8,128)S(1)}, f32[4,2,8,256]{3,2,1,0:T(8,128)S(1)}, u32[]{:S(2)}, u32[]{:S(2)}) collective-permute-start(f32[4,2,8,256]{3,2,1,0:T(8,128)S(1)} %get-tuple-element.313), channel_id=1, source_target_pairs={{0,28},{4,0},{8,4},{12,8},{16,12},{20,16},{24,20},{28,24},{1,29},{... | collective-permute-start | bytes 196616 | tf_op jit(solution)/shard_map/ppermute | solution.py:165
  22.0 6.1 %collective-permute-start.5 = (f32[4,4,8,256]{3,2,1,0:T(8,128)S(1)}, f32[4,4,8,256]{3,2,1,0:T(8,128)S(1)}, u32[]{:S(2)}, u32[]{:S(2)}) collective-permute-start(f32[4,4,8,256]{3,2,1,0:T(8,128)S(1)} %pad_maximum_fusion.4), channel_id=1, source_target_pairs={{0,24},{4,28},{8,0},{12,4},{16,8},{20,12},{24,16},{28,20},{1,25},{... | collective-permute-start | bytes 393224 | tf_op jit(solution)/shard_map/ppermute | solution.py:165
  28.1 9.6 %collective-permute-start.6 = (f32[4,8,8,256]{3,2,1,0:T(8,128)S(1)}, f32[4,8,8,256]{3,2,1,0:T(8,128)S(1)}, u32[]{:S(2)}, u32[]{:S(2)}) collective-permute-start(f32[4,8,8,256]{3,2,1,0:T(8,128)S(1)} %pad_maximum_fusion.3), channel_id=1, source_target_pairs={{0,16},{4,20},{8,24},{12,28},{16,0},{20,4},{24,8},{28,12},{1,17},{... | collective-permute-start | bytes 786440 | tf_op jit(solution)/shard_map/ppermute | solution.py:165
